TPU v7x, 32 devices: a whole 2x2x4 slice. The times are simulated.
32 devices in a mesh: rep: 8 (over z, x), shard: 4 (over y, core).
Axes of the slice: x: 2, y: 2, z: 4, core: 2. Of those that a mesh axis runs over, the one named last changes fastest.
Arguments:
- tokens: bfloat16 [49152, 960], P(('rep', 'shard')), may hold values from -6 to 6
- lengths: int32 [32], P(('rep', 'shard')), may hold values from 1024 to 1536, as said below
- cotangent: bfloat16 [49152, 960], P(('rep', 'shard')), may hold values from -6 to 6
- w_query: bfloat16 [960, 960], P('shard'), may hold values from -0.1875 to 0.1875
- w_key: bfloat16 [960, 320], P('shard'), may hold values from -0.1875 to 0.1875
- w_value: bfloat16 [960, 320], P('shard'), may hold values from -0.1875 to 0.1875
- w_out: bfloat16 [960, 960], P('shard'), may hold values from -0.5 to 0.5
- w_gate: bfloat16 [960, 2560], P('shard'), may hold values from -0.1875 to 0.1875
- w_up: bfloat16 [960, 2560], P('shard'), may hold values from -0.1875 to 0.1875
- w_down: bfloat16 [2560, 960], P('shard'), may hold values from -0.125 to 0.125
- gain_attn: bfloat16 [960], P('shard'), may hold values from 0.5 to 1.5
- gain_ffn: bfloat16 [960], P('shard'), may hold values from 0.5 to 1.5
Outputs:
- output: float32 [49152, 960], P(('rep', 'shard'))
- grad_tokens: float32 [49152, 960], P(('rep', 'shard'))
- grad_query: float32 [960, 960], P('shard')
- grad_key: float32 [960, 320], P('shard')
- grad_value: float32 [960, 320], P('shard')
- grad_outproj: float32 [960, 960], P('shard')
- grad_gate: float32 [960, 2560], P('shard')
- grad_up: float32 [960, 2560], P('shard')
- grad_down: float32 [2560, 960], P('shard')
- grad_gain_attn: float32 [960], P('shard')
- grad_gain_ffn: float32 [960], P('shard')
Inputs may be any that keep to these rules, and one draw needn't show every extreme that they name: `lengths`: some block holds a sequence of 1536 tokens and some one of 1024.
All inputs are finite; a program needn't handle non-finite values.
Results may differ from a plain program's by a relative error of at most 0.017.
Values may be sent and summed in bfloat16 or wider, within the bound.
A program may use at most 320 MiB of HBM per device.

v0:
```python
import jax
import jax.numpy as jnp
from jax import lax
from jax.sharding import PartitionSpec as P

D = 960
HEADS = 15
KV_HEADS = 5
HEAD_DIM = 64
QBLK = 512


EPS = 1e-05
THETA = 10000.0
NEGATIVE = -1e30


def rope_tables(row_count):
    half = HEAD_DIM // 2
    position = jnp.arange(row_count, dtype=jnp.float32)
    frequency = THETA ** (-jnp.arange(half, dtype=jnp.float32) * 2.0 / HEAD_DIM)
    angle = position[:, None] * frequency[None, :]
    return (jnp.cos(angle)[:, None, :], jnp.sin(angle)[:, None, :])


def rotate(tensor, cosine, sine, direction):
    half = HEAD_DIM // 2
    first_half = tensor[..., :half]
    second_half = tensor[..., half:]
    return jnp.concatenate(
        [
            first_half * cosine - direction * second_half * sine,
            second_half * cosine + direction * first_half * sine,
        ],
        -1,
    )


def outer(left, right):
    return lax.dot_general(
        left, right, (((0,), (0,)), ((), ())), preferred_element_type=jnp.float32
    )


def backward_product(grad_rows, weight):
    return lax.dot_general(
        grad_rows, weight, (((1,), (1,)), ((), ())), preferred_element_type=jnp.float32
    )


def rms_norm(inputs, gain):
    scale_row = lax.rsqrt(jnp.mean(inputs * inputs, -1, keepdims=True) + EPS)
    normed = inputs * scale_row
    return (normed, scale_row, (normed * gain).astype(jnp.bfloat16))


def rms_back(grad_rows, normed, scale_row, gain):
    gain_grad = jnp.sum(grad_rows * normed, 0)
    weighted = grad_rows * gain
    return (
        gain_grad,
        scale_row * (weighted - normed * jnp.mean(weighted * normed, -1, keepdims=True)),
    )


def score_block(query_block, key_rot, first_row):
    row_count = key_rot.shape[0]
    scores = jnp.einsum(
        "qgrd,kgd->grqk", query_block, key_rot, preferred_element_type=jnp.float32
    ) * HEAD_DIM ** (-0.5)
    query_pos = first_row + lax.iota(jnp.int32, QBLK)
    key_pos = lax.iota(jnp.int32, row_count)
    return jnp.where(key_pos[None, :] <= query_pos[:, None], scores, NEGATIVE)


def attend_forward(query_rot, key_rot, value_low, block_count):
    row_count = query_rot.shape[0]
    group_size = HEADS // KV_HEADS

    def visit(block_index, state_now):
        outputs, log_sums = state_now
        first_row = block_index * QBLK
        query_block = lax.dynamic_slice_in_dim(query_rot, first_row, QBLK, 0)
        scores = score_block(query_block, key_rot, first_row)
        row_max = jnp.max(scores, -1, keepdims=True)
        raised = jnp.exp(scores - row_max)
        summed = jnp.sum(raised, -1, keepdims=True)
        attn_prob = (raised / summed).astype(jnp.bfloat16)
        block_out = jnp.einsum(
            "grqk,kgd->qgrd", attn_prob, value_low, preferred_element_type=jnp.float32
        ).reshape(QBLK, D)
        block_log = (row_max + jnp.log(summed))[..., 0]
        outputs = lax.dynamic_update_slice_in_dim(outputs, block_out, first_row, 0)
        log_sums = lax.dynamic_update_slice_in_dim(log_sums, block_log, first_row, 2)
        return (outputs, log_sums)

    initial = (
        jnp.zeros((row_count, D), jnp.float32),
        jnp.zeros((KV_HEADS, group_size, row_count), jnp.float32),
    )
    return lax.fori_loop(0, block_count, visit, initial)


def attend_backward(query_rot, key_rot, value_low, grad_attn, log_sums, block_count):
    row_count = query_rot.shape[0]

    def visit(block_index, state_now):
        grad_query, grad_key, grad_val = state_now
        first_row = block_index * QBLK
        query_block = lax.dynamic_slice_in_dim(query_rot, first_row, QBLK, 0)
        grad_block = lax.dynamic_slice_in_dim(grad_attn, first_row, QBLK, 0)
        block_log = lax.dynamic_slice_in_dim(log_sums, first_row, QBLK, 2)
        scores = score_block(query_block, key_rot, first_row)
        attn_prob = jnp.exp(scores - block_log[..., None])
        prob_low = attn_prob.astype(jnp.bfloat16)
        grad_prob = jnp.einsum(
            "qgrd,kgd->grqk", grad_block, value_low, preferred_element_type=jnp.float32
        )
        centre = jnp.sum(attn_prob * grad_prob, -1, keepdims=True)
        grad_score = (attn_prob * (grad_prob - centre) * HEAD_DIM ** (-0.5)).astype(jnp.bfloat16)
        block_query = jnp.einsum(
            "grqk,kgd->qgrd", grad_score, key_rot, preferred_element_type=jnp.float32
        ).reshape(QBLK, D)
        grad_query = lax.dynamic_update_slice_in_dim(grad_query, block_query, first_row, 0)
        grad_key = grad_key + jnp.einsum(
            "grqk,qgrd->kgd", grad_score, query_block, preferred_element_type=jnp.float32
        )
        grad_val = grad_val + jnp.einsum(
            "grqk,qgrd->kgd", prob_low, grad_block, preferred_element_type=jnp.float32
        )
        return (grad_query, grad_key, grad_val)

    initial = (
        jnp.zeros((row_count, D), jnp.float32),
        jnp.zeros((row_count, KV_HEADS, HEAD_DIM), jnp.float32),
        jnp.zeros((row_count, KV_HEADS, HEAD_DIM), jnp.float32),
    )
    return lax.fori_loop(0, block_count, visit, initial)


def shards(
    tokens,
    lengths,
    cotangent,
    w_query,
    w_key,
    w_value,
    w_out,
    w_gate,
    w_up,
    w_down,
    gain_attn,
    gain_ffn,
):
    row_count = tokens.shape[0]
    group_size = HEADS // KV_HEADS
    length = lengths[0]
    live_mask = (lax.iota(jnp.int32, row_count) < length).astype(jnp.float32)[:, None]
    gathered = (
        lax.all_gather(w_query, "shard", axis=0, tiled=True),
        lax.all_gather(w_key, "shard", axis=0, tiled=True),
        lax.all_gather(w_value, "shard", axis=0, tiled=True),
        lax.all_gather(w_out, "shard", axis=0, tiled=True),
        lax.all_gather(w_gate, "shard", axis=0, tiled=True),
        lax.all_gather(w_up, "shard", axis=0, tiled=True),
        lax.all_gather(w_down, "shard", axis=0, tiled=True),
        lax.all_gather(gain_attn, "shard", axis=0, tiled=True),
        lax.all_gather(gain_ffn, "shard", axis=0, tiled=True),
    )
    (
        query_full,
        key_full,
        value_full,
        out_full,
        gate_full,
        up_full,
        down_full,
        gain_one,
        gain_two,
    ) = gathered
    inputs = tokens.astype(jnp.float32)
    normed_one, scale_one, hidden_one = rms_norm(inputs, gain_one.astype(jnp.float32))
    cosine, sine = rope_tables(row_count)
    queries = jnp.dot(hidden_one, query_full, preferred_element_type=jnp.float32).reshape(
        row_count, HEADS, HEAD_DIM
    )
    keys_raw = jnp.dot(hidden_one, key_full, preferred_element_type=jnp.float32).reshape(
        row_count, KV_HEADS, HEAD_DIM
    )
    values_low = (
        jnp.dot(hidden_one, value_full, preferred_element_type=jnp.float32)
        .astype(jnp.bfloat16)
        .reshape(row_count, KV_HEADS, HEAD_DIM)
    )
    query_rot = (
        rotate(queries, cosine, sine, 1.0)
        .astype(jnp.bfloat16)
        .reshape(row_count, KV_HEADS, group_size, HEAD_DIM)
    )
    key_rot = rotate(keys_raw, cosine, sine, 1.0).astype(jnp.bfloat16)
    block_count = row_count // QBLK
    attn_out, log_sums = attend_forward(query_rot, key_rot, values_low, block_count)
    attn_low = attn_out.astype(jnp.bfloat16)
    mixed = inputs + jnp.dot(attn_low, out_full, preferred_element_type=jnp.float32)
    normed_two, scale_two, hidden_two = rms_norm(mixed, gain_two.astype(jnp.float32))
    gate = jnp.dot(hidden_two, gate_full, preferred_element_type=jnp.float32)
    up_proj = jnp.dot(hidden_two, up_full, preferred_element_type=jnp.float32)
    sigmoid_gate = jax.nn.sigmoid(gate)
    activated = gate * sigmoid_gate
    product_low = (activated * up_proj).astype(jnp.bfloat16)
    output = (
        mixed + jnp.dot(product_low, down_full, preferred_element_type=jnp.float32)
    ) * live_mask
    back_weights = (
        lax.all_gather(w_query, "shard", axis=0, tiled=True),
        lax.all_gather(w_key, "shard", axis=0, tiled=True),
        lax.all_gather(w_value, "shard", axis=0, tiled=True),
        lax.all_gather(w_out, "shard", axis=0, tiled=True),
        lax.all_gather(w_gate, "shard", axis=0, tiled=True),
        lax.all_gather(w_up, "shard", axis=0, tiled=True),
        lax.all_gather(w_down, "shard", axis=0, tiled=True),
        lax.all_gather(gain_attn, "shard", axis=0, tiled=True),
        lax.all_gather(gain_ffn, "shard", axis=0, tiled=True),
    )
    (
        query_back,
        key_back,
        value_back,
        out_back,
        gate_back,
        up_back,
        down_back,
        gain_one_back,
        gain_two_back,
    ) = back_weights
    grad_rows = cotangent.astype(jnp.float32) * live_mask
    grad_low = grad_rows.astype(jnp.bfloat16)
    grad_down_w = outer(product_low, grad_low)
    grad_product = backward_product(grad_low, down_back).astype(jnp.bfloat16).astype(jnp.float32)
    silu_slope = sigmoid_gate * (1.0 + gate * (1.0 - sigmoid_gate))
    grad_gate_act = (grad_product * up_proj * silu_slope).astype(jnp.bfloat16)
    grad_up_act = (grad_product * activated).astype(jnp.bfloat16)
    grad_gate_w = outer(hidden_two, grad_gate_act)
    grad_up_w = outer(hidden_two, grad_up_act)
    grad_hidden_two = backward_product(grad_gate_act, gate_back) + backward_product(
        grad_up_act, up_back
    )
    grad_gain_two, grad_norm_two = rms_back(
        grad_hidden_two, normed_two, scale_two, gain_two_back.astype(jnp.float32)
    )
    grad_mixed = grad_rows + grad_norm_two
    grad_branch = grad_mixed.astype(jnp.bfloat16)
    grad_out_w = outer(attn_low, grad_branch)
    grad_attn = (
        backward_product(grad_branch, out_back)
        .astype(jnp.bfloat16)
        .reshape(row_count, KV_HEADS, group_size, HEAD_DIM)
    )
    grad_query_rot, grad_key_rot, grad_val_sum = attend_backward(
        query_rot, key_rot, values_low, grad_attn, log_sums, block_count
    )
    grad_queries = (
        rotate(grad_query_rot.reshape(row_count, HEADS, HEAD_DIM), cosine, sine, -1.0)
        .reshape(row_count, D)
        .astype(jnp.bfloat16)
    )
    grad_keys = (
        rotate(grad_key_rot, cosine, sine, -1.0)
        .reshape(row_count, KV_HEADS * HEAD_DIM)
        .astype(jnp.bfloat16)
    )
    grad_values = grad_val_sum.reshape(row_count, KV_HEADS * HEAD_DIM).astype(jnp.bfloat16)
    grad_query_w = outer(hidden_one, grad_queries)
    grad_key_w = outer(hidden_one, grad_keys)
    grad_value_w = outer(hidden_one, grad_values)
    grad_hidden_one = (
        backward_product(grad_queries, query_back)
        + backward_product(grad_keys, key_back)
        + backward_product(grad_values, value_back)
    )
    grad_gain_one, grad_norm_one = rms_back(
        grad_hidden_one, normed_one, scale_one, gain_one_back.astype(jnp.float32)
    )
    grad_inputs = grad_mixed + grad_norm_one
    shares = (
        lax.psum_scatter(
            grad_query_w.astype(jnp.bfloat16), "shard", scatter_dimension=0, tiled=True
        ).astype(jnp.float32),
        lax.psum_scatter(
            grad_key_w.astype(jnp.bfloat16), "shard", scatter_dimension=0, tiled=True
        ).astype(jnp.float32),
        lax.psum_scatter(
            grad_value_w.astype(jnp.bfloat16), "shard", scatter_dimension=0, tiled=True
        ).astype(jnp.float32),
        lax.psum_scatter(
            grad_out_w.astype(jnp.bfloat16), "shard", scatter_dimension=0, tiled=True
        ).astype(jnp.float32),
        lax.psum_scatter(
            grad_gate_w.astype(jnp.bfloat16), "shard", scatter_dimension=0, tiled=True
        ).astype(jnp.float32),
        lax.psum_scatter(
            grad_up_w.astype(jnp.bfloat16), "shard", scatter_dimension=0, tiled=True
        ).astype(jnp.float32),
        lax.psum_scatter(
            grad_down_w.astype(jnp.bfloat16), "shard", scatter_dimension=0, tiled=True
        ).astype(jnp.float32),
        lax.psum_scatter(
            grad_gain_one.astype(jnp.bfloat16), "shard", scatter_dimension=0, tiled=True
        ).astype(jnp.float32),
        lax.psum_scatter(
            grad_gain_two.astype(jnp.bfloat16), "shard", scatter_dimension=0, tiled=True
        ).astype(jnp.float32),
    )
    totals = lax.psum(
        (
            shares[0],
            shares[1],
            shares[2],
            shares[3],
            shares[4],
            shares[5],
            shares[6],
            shares[7],
            shares[8],
        ),
        "rep",
    )
    return (
        output,
        grad_inputs,
        totals[0],
        totals[1],
        totals[2],
        totals[3],
        totals[4],
        totals[5],
        totals[6],
        totals[7],
        totals[8],
    )


def solution(mesh):
    placed = (
        P(("rep", "shard"), None),
        P(("rep", "shard")),
        P(("rep", "shard"), None),
        P("shard", None),
        P("shard", None),
        P("shard", None),
        P("shard", None),
        P("shard", None),
        P("shard", None),
        P("shard", None),
        P("shard"),
        P("shard"),
    )
    return jax.shard_map(
        shards,
        mesh=mesh,
        in_specs=placed,
        out_specs=(
            P(("rep", "shard"), None),
            P(("rep", "shard"), None),
            P("shard", None),
            P("shard", None),
            P("shard", None),
            P("shard", None),
            P("shard", None),
            P("shard", None),
            P("shard", None),
            P("shard"),
            P("shard"),
        ),
        check_vma=False,
    )
```

profile of v0, /device:TPU:0, one launch (start us, length us, event | category | flops | bytes accessed | tf_op | source)
XLA Modules:
  0.0 1586.0 jit_solution(1472852711692245336)
XLA Ops:
  14.9 8.4 all-reduce.6
  26.6 10.5 all-gather
  38.5 2.6 reshape.161
  41.0 8.4 all-gather.1
  50.8 2.6 reshape.163
  53.4 3.4 convolution_convert_fusion.5
  58.5 6.1 fusion.75
  67.4 186.6 %while.33 = (s32[]{:T(128)}, bf16[1536,960]{0,1:T(8,128)(2,1)}, f32[5,3,1536]{2,1,0:T(4,128)S(1)}, bf16[1536,5,3,64]{0,3,2,1:T(8,128)(2,1)}, bf16[1536,5,64]{0,2...) while((s32[]{:T(128)}, bf16[1536,960]{0,1:T(8,128)(2,1)}, ...), condition=%wide.region_4.5_spmd, body=%wide.region_1.4_spmd.sunk | while | flops 3162235904 | bytes 150882464 | solution.py:101
  68.1 19.5 %bitcast_reduce_fusion.2 = (f32[5,3,512]{2,1,0:T(4,128)S(1)}, f32[5,512,3,1536]{3,1,2,0:T(8,128)}) fusion(pred[512,1536]{1,0:T(8,128)(4,1)S(1)} %iota_compare_fusion.5, bf16[1536,5,64]{0,2,1:T(8,128)(2,1)S(1)} %get-tuple-element.503, bf16[1536,5,3,64]{0,3,2,1:T(8,128)(2,1)} %get-tuple-element.502, s32[]{:T(128)S(6)} %select_n.63), kind=kOutput, calls=%fused_computation.1.clone.1 | convolution fusion | flops 1545331200 | bytes 49969156 | tf_op jit(solution)/shard_map/while/body/eval_jaxpr/qgrd,kgd->grqk/dot_general | solution.py:68
  87.6 21.1 %fusion.133 = f32[5,3,512]{2,1,0:T(4,128)S(1)} fusion(f32[5,512,3,1536]{3,1,2,0:T(8,128)} %get-tuple-element.468, f32[5,3,512]{2,1,0:T(4,128)S(1)} %get-tuple-element.469, pred[512,1536]{1,0:T(8,128)(4,1)S(1)} %iota_compare_fusion.5), kind=kLoop, calls=%fused_computation.5.clone.1 | loop fusion | flops 47178240 | bytes 48033792 | tf_op jit(solution)/shard_map/while/body/eval_jaxpr/reduce_sum | solution.py:87
  108.8 20.2 %fusion.134 = bf16[5,3,512,64]{2,3,1,0:T(8,128)(2,1)S(1)} fusion(f32[5,512,3,1536]{3,1,2,0:T(8,128)} %get-tuple-element.468, f32[5,3,512]{2,1,0:T(4,128)S(1)} %fusion.133, f32[5,3,512]{2,1,0:T(4,128)S(1)} %get-tuple-element.469, pred[512,1536]{1,0:T(8,128)(4,1)S(1)} %iota_compare_fusion.5, bf16[1536,5,64]{0,2,1:T(8,128)(2,1)S(1)} %get-tuple-element.504), kind=kOutput, calls=%fused_computation.6.clone.1 | convolution fusion | flops 1568931840 | bytes 49999872 | tf_op jit(solution)/shard_map/while/body/eval_jaxpr/grqk,kgd->qgrd/dot_general | solution.py:89
  130.7 20.0 %bitcast_reduce_fusion.2 = (f32[5,3,512]{2,1,0:T(4,128)S(1)}, f32[5,512,3,1536]{3,1,2,0:T(8,128)}) fusion(pred[512,1536]{1,0:T(8,128)(4,1)S(1)} %iota_compare_fusion.5, bf16[1536,5,64]{0,2,1:T(8,128)(2,1)S(1)} %get-tuple-element.503, bf16[1536,5,3,64]{0,3,2,1:T(8,128)(2,1)} %get-tuple-element.502, s32[]{:T(128)S(6)} %select_n.63), kind=kOutput, calls=%fused_computation.1.clone.1 | convolution fusion | flops 1545331200 | bytes 49969156 | tf_op jit(solution)/shard_map/while/body/eval_jaxpr/qgrd,kgd->grqk/dot_general | solution.py:68
  150.7 22.0 %fusion.133 = f32[5,3,512]{2,1,0:T(4,128)S(1)} fusion(f32[5,512,3,1536]{3,1,2,0:T(8,128)} %get-tuple-element.468, f32[5,3,512]{2,1,0:T(4,128)S(1)} %get-tuple-element.469, pred[512,1536]{1,0:T(8,128)(4,1)S(1)} %iota_compare_fusion.5), kind=kLoop, calls=%fused_computation.5.clone.1 | loop fusion | flops 47178240 | bytes 48033792 | tf_op jit(solution)/shard_map/while/body/eval_jaxpr/reduce_sum | solution.py:87
  172.7 19.0 %fusion.134 = bf16[5,3,512,64]{2,3,1,0:T(8,128)(2,1)S(1)} fusion(f32[5,512,3,1536]{3,1,2,0:T(8,128)} %get-tuple-element.468, f32[5,3,512]{2,1,0:T(4,128)S(1)} %fusion.133, f32[5,3,512]{2,1,0:T(4,128)S(1)} %get-tuple-element.469, pred[512,1536]{1,0:T(8,128)(4,1)S(1)} %iota_compare_fusion.5, bf16[1536,5,64]{0,2,1:T(8,128)(2,1)S(1)} %get-tuple-element.504), kind=kOutput, calls=%fused_computation.6.clone.1 | convolution fusion | flops 1568931840 | bytes 49999872 | tf_op jit(solution)/shard_map/while/body/eval_jaxpr/grqk,kgd->qgrd/dot_general | solution.py:89
  193.2 19.3 %bitcast_reduce_fusion.2 = (f32[5,3,512]{2,1,0:T(4,128)S(1)}, f32[5,512,3,1536]{3,1,2,0:T(8,128)}) fusion(pred[512,1536]{1,0:T(8,128)(4,1)S(1)} %iota_compare_fusion.5, bf16[1536,5,64]{0,2,1:T(8,128)(2,1)S(1)} %get-tuple-element.503, bf16[1536,5,3,64]{0,3,2,1:T(8,128)(2,1)} %get-tuple-element.502, s32[]{:T(128)S(6)} %select_n.63), kind=kOutput, calls=%fused_computation.1.clone.1 | convolution fusion | flops 1545331200 | bytes 49969156 | tf_op jit(solution)/shard_map/while/body/eval_jaxpr/qgrd,kgd->grqk/dot_general | solution.py:68
  212.5 21.1 %fusion.133 = f32[5,3,512]{2,1,0:T(4,128)S(1)} fusion(f32[5,512,3,1536]{3,1,2,0:T(8,128)} %get-tuple-element.468, f32[5,3,512]{2,1,0:T(4,128)S(1)} %get-tuple-element.469, pred[512,1536]{1,0:T(8,128)(4,1)S(1)} %iota_compare_fusion.5), kind=kLoop, calls=%fused_computation.5.clone.1 | loop fusion | flops 47178240 | bytes 48033792 | tf_op jit(solution)/shard_map/while/body/eval_jaxpr/reduce_sum | solution.py:87
  233.6 19.0 %fusion.134 = bf16[5,3,512,64]{2,3,1,0:T(8,128)(2,1)S(1)} fusion(f32[5,512,3,1536]{3,1,2,0:T(8,128)} %get-tuple-element.468, f32[5,3,512]{2,1,0:T(4,128)S(1)} %fusion.133, f32[5,3,512]{2,1,0:T(4,128)S(1)} %get-tuple-element.469, pred[512,1536]{1,0:T(8,128)(4,1)S(1)} %iota_compare_fusion.5, bf16[1536,5,64]{0,2,1:T(8,128)(2,1)S(1)} %get-tuple-element.504), kind=kOutput, calls=%fused_computation.6.clone.1 | convolution fusion | flops 1568931840 | bytes 49999872 | tf_op jit(solution)/shard_map/while/body/eval_jaxpr/grqk,kgd->qgrd/dot_general | solution.py:89
  254.1 7.1 multiply_reduce_fusion.2
  266.0 14.4 fusion.78
  280.4 25.0 %convolution_convert_fusion = bf16[1536,2560]{1,0:T(8,128)(2,1)} fusion(bf16[2560,960]{0,1:T(8,128)(2,1)} %all-gather.16.cloned.1.call-done, bf16[1536,960]{0,1:T(8,128)(2,1)} %param.18, f32[1536]{0:T(1024)S(1)} %copy-done.23), kind=kOutput, calls=%fused_computation.63 | convolution fusion | flops 7558103040 | bytes 15734784 | tf_op jit(solution)/shard_map/dot_general | solution.py:46
  305.4 24.1 %fusion.45 = (bf16[1536,2560]{1,0:T(8,128)(2,1)S(1)}, bf16[1536,2560]{1,0:T(8,128)(2,1)}, bf16[1536,2560]{1,0:T(8,128)(2,1)}) fusion(bf16[1536,2560]{1,0:T(8,128)(2,1)} %convolution_convert_fusion, f32[1536,2560]{1,0:T(8,128)} %fusion.78, bf16[1536,960]{0,1:T(8,128)(2,1)} %multiply_convert_fusion.1, bf16[960,2560]{1,0:T(8,128)(2,1)} %all-gather.14.cloned.1.call-done), kind=kOutput, calls=%fused_computation.58 | convolution fusion | flops 7612661760 | bytes 55050240 | tf_op jit(solution)/shard_map/dot_general | solution.py:207
  329.5 13.3 fusion.79
  342.8 13.3 multiply_reduce_fusion
  356.1 3.7 multiply_add_fusion
  359.9 4.6 convolution_convert_fusion.4
  364.5 3.2 broadcast.137
  367.7 541.5 %while.34 = (s32[]{:T(128)}, f32[1536,960]{0,1:T(8,128)}, f32[1536,5,64]{0,2,1:T(8,128)}, f32[1536,5,64]{0,2,1:T(8,128)S(1)}, bf16[1536,5,3,64]{0,3,2,1:T(8,128)...) while((s32[]{:T(128)}, f32[1536,960]{0,1:T(8,128)}, ...), condition=%wide.region_9.0_spmd.clone, body=%wide.region_7.0_spmd.clone.sunk | while | flops 7717669376 | bytes 450918624 | solution.py:138
  369.5 21.9 %fusion.143 = f32[5,3,512,1536]{3,2,1,0:T(8,128)} fusion(f32[5,3,512]{2,1,0:T(4,128)S(1)} %constant_dynamic-slice_fusion.2, pred[512,1536]{1,0:T(8,128)(4,1)} %iota_compare_fusion.6, bf16[1536,5,64]{0,2,1:T(8,128)(2,1)S(1)} %get-tuple-element.540, bf16[1536,5,3,64]{0,3,2,1:T(8,128)(2,1)} %get-tuple-element.539, s32[]{:T(128)S(6)} %select_n.65), kind=kOutput, calls=%fused_computation.25.clone.1 | convolution fusion | flops 1545338880 | bytes 49969156 | tf_op jit(solution)/shard_map/while/body/eval_jaxpr/qgrd,kgd->grqk/dot_general | solution.py:68
  391.4 16.6 %fusion.147 = f32[1536,5,64]{0,2,1:T(8,128)S(1)} fusion(f32[5,3,512,1536]{3,2,1,0:T(8,128)} %fusion.143, f32[1536,5,64]{0,2,1:T(8,128)S(1)} %get-tuple-element.525, pred[]{:T(512)S(6)} %compare.3, bf16[1536,5,3,64]{0,3,2,1:T(8,128)(2,1)} %get-tuple-element.542, s32[]{:T(128)S(6)} %select_n.65), kind=kOutput, calls=%fused_computation.34.clone.1 | convolution fusion | flops 1522728960 | bytes 52101124 | tf_op jit(solution)/shard_map/while/body/eval_jaxpr/grqk,qgrd->kgd/dot_general | solution.py:128
  408.1 19.5 %fusion.144 = f32[5,512,3,1536]{3,1,2,0:T(8,128)} fusion(bf16[1536,5,64]{0,2,1:T(8,128)(2,1)S(1)} %copy-done.4, bf16[1536,5,3,64]{0,3,2,1:T(8,128)(2,1)} %get-tuple-element.542, s32[]{:T(128)S(6)} %select_n.65), kind=kOutput, calls=%fused_computation.36.clone.1 | convolution fusion | flops 1509949440 | bytes 49152004 | tf_op jit(solution)/shard_map/while/body/eval_jaxpr/qgrd,kgd->grqk/dot_general | solution.py:116
  427.6 59.0 %fusion.146 = f32[1536,5,64]{0,2,1:T(8,128)} fusion(f32[5,3,512,1536]{3,2,1,0:T(8,128)} %fusion.143, f32[5,512,3,1536]{3,1,2,0:T(8,128)} %fusion.144, f32[1536,5,64]{0,2,1:T(8,128)} %get-tuple-element.524, pred[]{:T(512)S(6)} %compare.3, bf16[1536,5,3,64]{0,3,2,1:T(8,128)(2,1)} %get-tuple-element.539, s32[]{:T(128)S(6)} %select_n.65), kind=kOutput, calls=%fused_computation.35.clone.2 | convolution fusion | flops 1569924096 | bytes 193658880 | tf_op jit(solution)/shard_map/while/body/eval_jaxpr/grqk,qgrd->kgd/dot_general | solution.py:125
  486.6 58.5 %fusion.145 = f32[5,3,512,64]{2,3,1,0:T(8,128)} fusion(f32[5,3,512,1536]{3,2,1,0:T(8,128)} %fusion.143, f32[5,512,3,1536]{3,1,2,0:T(8,128)} %fusion.144, bf16[1536,5,64]{0,2,1:T(8,128)(2,1)S(1)} %get-tuple-element.540), kind=kOutput, calls=%fused_computation.30.clone.1 | convolution fusion | flops 1568941056 | bytes 97320960 | tf_op jit(solution)/shard_map/while/body/eval_jaxpr/grqk,kgd->qgrd/dot_general | solution.py:121
  545.1 3.0 constant_dynamic-update-slice_fusion.5
  549.6 21.9 %fusion.143 = f32[5,3,512,1536]{3,2,1,0:T(8,128)} fusion(f32[5,3,512]{2,1,0:T(4,128)S(1)} %constant_dynamic-slice_fusion.2, pred[512,1536]{1,0:T(8,128)(4,1)} %iota_compare_fusion.6, bf16[1536,5,64]{0,2,1:T(8,128)(2,1)S(1)} %get-tuple-element.540, bf16[1536,5,3,64]{0,3,2,1:T(8,128)(2,1)} %get-tuple-element.539, s32[]{:T(128)S(6)} %select_n.65), kind=kOutput, calls=%fused_computation.25.clone.1 | convolution fusion | flops 1545338880 | bytes 49969156 | tf_op jit(solution)/shard_map/while/body/eval_jaxpr/qgrd,kgd->grqk/dot_general | solution.py:68
  571.5 16.6 %fusion.147 = f32[1536,5,64]{0,2,1:T(8,128)S(1)} fusion(f32[5,3,512,1536]{3,2,1,0:T(8,128)} %fusion.143, f32[1536,5,64]{0,2,1:T(8,128)S(1)} %get-tuple-element.525, pred[]{:T(512)S(6)} %compare.3, bf16[1536,5,3,64]{0,3,2,1:T(8,128)(2,1)} %get-tuple-element.542, s32[]{:T(128)S(6)} %select_n.65), kind=kOutput, calls=%fused_computation.34.clone.1 | convolution fusion | flops 1522728960 | bytes 52101124 | tf_op jit(solution)/shard_map/while/body/eval_jaxpr/grqk,qgrd->kgd/dot_general | solution.py:128
  588.1 19.5 %fusion.144 = f32[5,512,3,1536]{3,1,2,0:T(8,128)} fusion(bf16[1536,5,64]{0,2,1:T(8,128)(2,1)S(1)} %copy-done.4, bf16[1536,5,3,64]{0,3,2,1:T(8,128)(2,1)} %get-tuple-element.542, s32[]{:T(128)S(6)} %select_n.65), kind=kOutput, calls=%fused_computation.36.clone.1 | convolution fusion | flops 1509949440 | bytes 49152004 | tf_op jit(solution)/shard_map/while/body/eval_jaxpr/qgrd,kgd->grqk/dot_general | solution.py:116
  607.6 59.4 %fusion.146 = f32[1536,5,64]{0,2,1:T(8,128)} fusion(f32[5,3,512,1536]{3,2,1,0:T(8,128)} %fusion.143, f32[5,512,3,1536]{3,1,2,0:T(8,128)} %fusion.144, f32[1536,5,64]{0,2,1:T(8,128)} %get-tuple-element.524, pred[]{:T(512)S(6)} %compare.3, bf16[1536,5,3,64]{0,3,2,1:T(8,128)(2,1)} %get-tuple-element.539, s32[]{:T(128)S(6)} %select_n.65), kind=kOutput, calls=%fused_computation.35.clone.2 | convolution fusion | flops 1569924096 | bytes 193658880 | tf_op jit(solution)/shard_map/while/body/eval_jaxpr/grqk,qgrd->kgd/dot_general | solution.py:125
  667.0 58.5 %fusion.145 = f32[5,3,512,64]{2,3,1,0:T(8,128)} fusion(f32[5,3,512,1536]{3,2,1,0:T(8,128)} %fusion.143, f32[5,512,3,1536]{3,1,2,0:T(8,128)} %fusion.144, bf16[1536,5,64]{0,2,1:T(8,128)(2,1)S(1)} %get-tuple-element.540), kind=kOutput, calls=%fused_computation.30.clone.1 | convolution fusion | flops 1568941056 | bytes 97320960 | tf_op jit(solution)/shard_map/while/body/eval_jaxpr/grqk,kgd->qgrd/dot_general | solution.py:121
  725.5 3.1 constant_dynamic-update-slice_fusion.5
  730.0 21.9 %fusion.143 = f32[5,3,512,1536]{3,2,1,0:T(8,128)} fusion(f32[5,3,512]{2,1,0:T(4,128)S(1)} %constant_dynamic-slice_fusion.2, pred[512,1536]{1,0:T(8,128)(4,1)} %iota_compare_fusion.6, bf16[1536,5,64]{0,2,1:T(8,128)(2,1)S(1)} %get-tuple-element.540, bf16[1536,5,3,64]{0,3,2,1:T(8,128)(2,1)} %get-tuple-element.539, s32[]{:T(128)S(6)} %select_n.65), kind=kOutput, calls=%fused_computation.25.clone.1 | convolution fusion | flops 1545338880 | bytes 49969156 | tf_op jit(solution)/shard_map/while/body/eval_jaxpr/qgrd,kgd->grqk/dot_general | solution.py:68
  751.9 16.6 %fusion.147 = f32[1536,5,64]{0,2,1:T(8,128)S(1)} fusion(f32[5,3,512,1536]{3,2,1,0:T(8,128)} %fusion.143, f32[1536,5,64]{0,2,1:T(8,128)S(1)} %get-tuple-element.525, pred[]{:T(512)S(6)} %compare.3, bf16[1536,5,3,64]{0,3,2,1:T(8,128)(2,1)} %get-tuple-element.542, s32[]{:T(128)S(6)} %select_n.65), kind=kOutput, calls=%fused_computation.34.clone.1 | convolution fusion | flops 1522728960 | bytes 52101124 | tf_op jit(solution)/shard_map/while/body/eval_jaxpr/grqk,qgrd->kgd/dot_general | solution.py:128
  768.5 19.5 %fusion.144 = f32[5,512,3,1536]{3,1,2,0:T(8,128)} fusion(bf16[1536,5,64]{0,2,1:T(8,128)(2,1)S(1)} %copy-done.4, bf16[1536,5,3,64]{0,3,2,1:T(8,128)(2,1)} %get-tuple-element.542, s32[]{:T(128)S(6)} %select_n.65), kind=kOutput, calls=%fused_computation.36.clone.1 | convolution fusion | flops 1509949440 | bytes 49152004 | tf_op jit(solution)/shard_map/while/body/eval_jaxpr/qgrd,kgd->grqk/dot_general | solution.py:116
  788.0 59.4 %fusion.146 = f32[1536,5,64]{0,2,1:T(8,128)} fusion(f32[5,3,512,1536]{3,2,1,0:T(8,128)} %fusion.143, f32[5,512,3,1536]{3,1,2,0:T(8,128)} %fusion.144, f32[1536,5,64]{0,2,1:T(8,128)} %get-tuple-element.524, pred[]{:T(512)S(6)} %compare.3, bf16[1536,5,3,64]{0,3,2,1:T(8,128)(2,1)} %get-tuple-element.539, s32[]{:T(128)S(6)} %select_n.65), kind=kOutput, calls=%fused_computation.35.clone.2 | convolution fusion | flops 1569924096 | bytes 193658880 | tf_op jit(solution)/shard_map/while/body/eval_jaxpr/grqk,qgrd->kgd/dot_general | solution.py:125
  847.4 58.5 %fusion.145 = f32[5,3,512,64]{2,3,1,0:T(8,128)} fusion(f32[5,3,512,1536]{3,2,1,0:T(8,128)} %fusion.143, f32[5,512,3,1536]{3,1,2,0:T(8,128)} %fusion.144, bf16[1536,5,64]{0,2,1:T(8,128)(2,1)S(1)} %get-tuple-element.540), kind=kOutput, calls=%fused_computation.30.clone.1 | convolution fusion | flops 1568941056 | bytes 97320960 | tf_op jit(solution)/shard_map/while/body/eval_jaxpr/grqk,kgd->qgrd/dot_general | solution.py:121
  905.9 3.1 constant_dynamic-update-slice_fusion.5
  912.0 3.1 convolution_convert_fusion.9
  916.5 3.5 convolution_convert_fusion.8
  921.2 8.3 convolution_convert_fusion.6
  929.7 3.8 subtract_convert_fusion
  935.4 4.5 convolution_convert_fusion.7
  940.0 12.5 convolution_convert_fusion.1
  952.5 7.8 copy.37
  960.4 12.7 convolution_convert_fusion.3
  973.2 12.8 convolution_convert_fusion.2
  986.7 3.3 fusion.80
  990.0 3.2 fusion.81
  993.3 5.3 fusion.57
  998.5 6.3 all-reduce.5
  1004.9 9.1 fusion.56
  1014.1 14.5 add_multiply_fusion
  1033.1 53.8 %reduce-scatter.26.cloned.1.call-done = bf16[640,960]{1,0:T(8,128)(2,1)} async-done(((bf16[2560,960]{1,0:T(8,128)(2,1)}), bf16[640,960]{1,0:T(8,128)(2,1)}) %reduce-scatter.26.cloned.1.call-update) | async-done | bytes 1228816
  1089.1 49.9 %reduce-scatter.18.cloned.1.call-done = bf16[240,2560]{1,0:T(8,128)(2,1)} async-done(((bf16[960,2560]{1,0:T(8,128)(2,1)}), bf16[240,2560]{1,0:T(8,128)(2,1)}) %reduce-scatter.18.cloned.1.call-update) | async-done | bytes 1228816 | tf_op jit(solution)/shard_map/reduce_scatter | solution.py:298
  1138.9 51.7 %reduce-scatter.20.cloned.1.call-done = bf16[240,2560]{1,0:T(8,128)(2,1)} async-done(((bf16[960,2560]{1,0:T(8,128)(2,1)}), bf16[240,2560]{1,0:T(8,128)(2,1)}) %reduce-scatter.20.cloned.1.call-update) | async-done | bytes 1228816 | tf_op jit(solution)/shard_map/reduce_scatter | solution.py:301
  1190.6 388.3 %all-reduce.8 = (f32[240,960]{1,0:T(8,128)}, f32[240,320]{0,1:T(8,128)}, f32[240,320]{0,1:T(8,128)}, f32[240,960]{1,0:T(8,128)}, f32[240,2560]{1,0:T(8,128)}, /*...) all-reduce(bf16[240,960]{1,0:T(8,128)(2,1)} %reduce-scatter.14.clon, ...), channel_id=1, replica_groups=mesh['rep'=8,'shard'=4] {'rep'}, use_global_device_ids=true, to_apply=%region_12.13 | all-reduce | flops 2458080 | bytes 14749440 | tf_op jit(solution)/shard_map/psum | solution.py:314
  (166 shorter events, 45.0 us)
Async XLA Ops:
  7.2 6.0 copy-start.25
  7.2 7.3 copy-start.30
  7.2 7.5 copy-start.31
  7.2 17.3 %copy-start.1 = (bf16[1536,960]{0,1:T(8,128)(2,1)S(1)}, bf16[1536,960]{0,1:T(8,128)(2,1)}, u32[]{:S(2)}) copy-start(bf16[1536,960]{0,1:T(8,128)(2,1)} %param.16) | copy-start | bytes 8847364
  7.2 19.4 %copy-start.17 = (bf16[240,320]{0,1:T(8,128)(2,1)S(1)}, bf16[240,320]{0,1:T(8,128)(2,1)}, u32[]{:S(2)}) copy-start(bf16[240,320]{0,1:T(8,128)(2,1)} %param.20) | copy-start | bytes 460804
  7.2 51.2 %all-gather.8.cloned.1.call-start = ((), (), s32[]{:S(2)}) async-start(), calls=%async_computation.7 | async-start | bytes 2457600 | tf_op jit(solution)/shard_map/all_gather | solution.py:160
  8.0 246.1 %all-gather.10.cloned.1.call-start = ((), (), s32[]{:S(2)}) async-start(), calls=%async_computation.8 | async-start | bytes 2457600 | tf_op jit(solution)/shard_map/all_gather | solution.py:163
  8.7 257.2 %all-gather.12.cloned.1.call-start = ((), (), s32[]{:S(2)}) async-start(), calls=%async_computation.9 | async-start | bytes 6144000 | tf_op jit(solution)/shard_map/all_gather | solution.py:164
  9.5 270.9 %all-gather.16.cloned.1.call-start = ((), (), s32[]{:S(2)}) async-start(), calls=%async_computation.11 | async-start | bytes 6144000 | tf_op jit(solution)/shard_map/all_gather | solution.py:166
  10.0 295.3 %all-gather.14.cloned.1.call-start = ((), (), s32[]{:S(2)}) async-start(), calls=%async_computation.10 | async-start | bytes 6144000 | tf_op jit(solution)/shard_map/all_gather | solution.py:165
  10.6 1017.9 %reduce-scatter.22.cloned.1.call-start = ((), (), s32[]{:S(2)}) async-start(), calls=%async_computation.16 | async-start | bytes 921600
  23.3 35.2 %copy-start.21 = (f32[960]{0:T(1024)}, f32[960]{0:T(1024)S(1)}, u32[]{:S(2)}) copy-start(f32[960]{0:T(1024)S(1)} %convert_element_type.150) | copy-start | bytes 11524
  25.1 33.3 %copy-start.18 = (f32[1536]{0:T(1024)}, f32[1536]{0:T(1024)S(1)}, u32[]{:S(2)}) copy-start(f32[1536]{0:T(1024)S(1)} %add_rsqrt_fusion.1) | copy-start | bytes 18436
  26.6 37.9 %copy-start.8 = (f32[1536,32]{0,1:T(8,128)}, f32[1536,32]{0,1:T(8,128)S(1)}, u32[]{:S(2)}) copy-start(f32[1536,32]{0,1:T(8,128)S(1)} %get-tuple-element.376) | copy-start | bytes 589828
  53.4 3.4 copy-start.15
  64.6 2.8 copy-start.3
  254.1 9.7 copy-start.20
  261.2 2.6 copy-start.5
  266.0 14.4 copy-start.23
  329.5 13.3 copy-start.32
  329.5 13.3 copy-start.27
  329.5 26.6 %slice-start = ((s8[5898240]{0:T(1024)(128)(4,1)}), s8[4194304]{0:T(1024)(128)(4,1)S(1)}, s32[]{:S(2)}) async-start(s8[5898240]{0:T(1024)(128)(4,1)} %bitcast.183), calls=%async_computation.19 | async-start | bytes 8388608
  342.8 13.3 slice-start.1
  356.1 3.8 copy-start.29
  359.9 4.6 copy-start.6
  364.5 3.2 copy-start
  367.7 541.5 %copy-start.9 = (f32[1536,32]{0,1:T(8,128)S(1)}, f32[1536,32]{0,1:T(8,128)}, u32[]{:S(2)}) copy-start(f32[1536,32]{0,1:T(8,128)} %copy-done.8) | copy-start | bytes 589828
  367.7 541.5 %copy-start.16 = (f32[1536,32]{0,1:T(8,128)S(1)}, f32[1536,32]{0,1:T(8,128)}, u32[]{:S(2)}) copy-start(f32[1536,32]{0,1:T(8,128)} %get-tuple-element.374) | copy-start | bytes 589828
  367.7 544.4 %copy-start.19 = (f32[1536]{0:T(1024)S(1)}, f32[1536]{0:T(1024)}, u32[]{:S(2)}) copy-start(f32[1536]{0:T(1024)} %copy-done.18) | copy-start | bytes 18436
  367.7 544.4 %copy-start.22 = (f32[960]{0:T(1024)S(1)}, f32[960]{0:T(1024)}, u32[]{:S(2)}) copy-start(f32[960]{0:T(1024)} %copy-done.21) | copy-start | bytes 11524
  391.4 16.6 %copy-start.4 = (bf16[1536,5,64]{0,2,1:T(8,128)(2,1)S(1)}, bf16[1536,5,64]{0,2,1:T(8,128)(2,1)}, u32[]{:S(2)}) copy-start(bf16[1536,5,64]{0,2,1:T(8,128)(2,1)} %get-tuple-element.543) | copy-start | bytes 2949124 | tf_op jit(solution)/shard_map/while
  571.5 16.6 %copy-start.4 = (bf16[1536,5,64]{0,2,1:T(8,128)(2,1)S(1)}, bf16[1536,5,64]{0,2,1:T(8,128)(2,1)}, u32[]{:S(2)}) copy-start(bf16[1536,5,64]{0,2,1:T(8,128)(2,1)} %get-tuple-element.543) | copy-start | bytes 2949124 | tf_op jit(solution)/shard_map/while
  751.9 16.6 %copy-start.4 = (bf16[1536,5,64]{0,2,1:T(8,128)(2,1)S(1)}, bf16[1536,5,64]{0,2,1:T(8,128)(2,1)}, u32[]{:S(2)}) copy-start(bf16[1536,5,64]{0,2,1:T(8,128)(2,1)} %get-tuple-element.543) | copy-start | bytes 2949124 | tf_op jit(solution)/shard_map/while
  911.1 0.9 copy-start.7
  916.3 113.3 %reduce-scatter.24.cloned.1.call-start = ((), (), s32[]{:S(2)}) async-start(), calls=%async_computation.17 | async-start | bytes 921600
  916.5 3.5 copy-start.10
  921.2 109.5 %reduce-scatter.16.cloned.1.call-start = ((), (), s32[]{:S(2)}) async-start(), calls=%async_computation.13 | async-start | bytes 2457600 | tf_op jit(solution)/shard_map/reduce_scatter | solution.py:295
  929.6 103.5 %reduce-scatter.14.cloned.1.call-start = ((), (), s32[]{:S(2)}) async-start(), calls=%async_computation.12 | async-start | bytes 2457600 | tf_op jit(solution)/shard_map/reduce_scatter | solution.py:286
  929.6 5.8 copy-start.2
  933.7 1.7 copy-start.12
  935.4 4.5 copy-start.24
  939.9 147.0 %reduce-scatter.26.cloned.1.call-start = ((), (), s32[]{:S(2)}) async-start(), calls=%async_computation.18 | async-start | bytes 6553600
  960.3 178.6 %reduce-scatter.18.cloned.1.call-start = ((), (), s32[]{:S(2)}) async-start(), calls=%async_computation.14 | async-start | bytes 6144000 | tf_op jit(solution)/shard_map/reduce_scatter | solution.py:298
  973.1 217.5 %reduce-scatter.20.cloned.1.call-start = ((), (), s32[]{:S(2)}) async-start(), calls=%async_computation.15 | async-start | bytes 6144000 | tf_op jit(solution)/shard_map/reduce_scatter | solution.py:301
  986.7 3.3 copy-start.13
  986.7 3.3 copy-start.28
  990.0 3.2 copy-start.11
  990.0 3.2 copy-start.14
  993.2 5.3 copy-start.26
Sparse Core Ops, SparseCore 0:
  9.6 27.7 all-gather.7
  39.0 21.6 all-gather.9
  62.3 38.5 all-gather.11
  102.3 38.5 all-gather.15
  142.3 38.5 all-gather.13
  916.5 23.0 reduce-scatter.21
  942.3 22.9 reduce-scatter.23
  968.4 30.6 reduce-scatter.15
  1002.4 30.6 reduce-scatter.13
  1035.5 51.3 reduce-scatter.25
  1089.7 49.1 reduce-scatter.17
  1141.4 49.1 reduce-scatter.19
where the time goes:
time: 1590 us
  matrix products  841 us (53%)
  blocking collectives  422 us (27%)
  waiting for transfers between devices  161 us (10%)
  other arithmetic  99.4 us (6%)
  local copies, waits for them, and re-layouts  44.3 us (3%)
  between operations  17 us (1%)
    psum x1, blocking collectives, shards(): lax.psum((shares[0], shares[1], shares[2], shares[3], shares[4], shares[5...  388 us
    dot_general x3, matrix products, visit(): jnp.einsum('grqk,qgrd->kgd', grad_score, query_block, preferred_element_t...  178 us
    dot_general x3, matrix products, visit(): jnp.einsum('grqk,kgd->qgrd', grad_score, key_rot, preferred_element_type=...  176 us
    dot_general x6, matrix products, score_block(): jnp.einsum('qgrd,kgd->grqk', query_block, key_rot, preferred_element_type...  124 us
    dot_general x7, matrix products, backward_product(): lax.dot_general(grad_rows, weight, (((1,), (1,)), ((), ())), preferred_el...  67.9 us
    reduce_sum x3, other arithmetic, visit(): summed = jnp.sum(raised, -1, keepdims=True)  64.2 us
    dot_general x3, matrix products, visit(): jnp.einsum('qgrd,kgd->grqk', grad_block, value_low, preferred_element_typ...  58.5 us
    dot_general x3, matrix products, visit(): jnp.einsum('grqk,kgd->qgrd', attn_prob, value_low, preferred_element_type...  58.1 us
  transfers between devices with their start and end apart: 12, of which 4 were waited for; matrix products, arithmetic and copies ran while one was open for 23% of the time, Pallas kernels for 0%

commit v1 on v0

v1 whole, which is shorter than its diff:
```python
import jax
import jax.numpy as jnp
from jax import lax
from jax.experimental import pallas as pl
from jax.experimental.pallas import tpu as pltpu
from jax.sharding import PartitionSpec as P

D = 960
HEADS = 15
KV_HEADS = 5
HEAD_DIM = 64
GROUP = HEADS // KV_HEADS
KV = KV_HEADS * HEAD_DIM
QB = 256
SCALE = HEAD_DIM ** (-0.5)
EPS = 1e-05
THETA = 10000.0
NEGATIVE = -1e30
VMEM = 48 * 1024 * 1024


def dot(left, right, contract):
    return lax.dot_general(
        left, right, ((contract[:1], contract[1:]), ((), ())), preferred_element_type=jnp.float32
    )


def diagonal(scores):
    keys = lax.broadcasted_iota(jnp.int32, scores.shape, 0)
    queries = lax.broadcasted_iota(jnp.int32, scores.shape, 1)
    return jnp.where(keys <= queries, scores, NEGATIVE)


def forward_kernel(q_ref, k_ref, v_ref, out_ref, log_ref):
    rows = q_ref.shape[1]
    key_rows = k_ref[...].T
    for start in range(0, rows, QB):
        stop = start + QB
        query = q_ref[:, start:stop]
        low = diagonal(dot(key_rows[start:stop], query, (1, 0)))
        top = jnp.max(low, 0, keepdims=True)
        if start:
            high = dot(key_rows[:start], query, (1, 0))
            top = jnp.maximum(top, jnp.max(high, 0, keepdims=True))
        low = jnp.exp(low - top)
        total = jnp.sum(low, 0, keepdims=True)
        mixed = dot(v_ref[:, start:stop], low.astype(jnp.bfloat16), (1, 0))
        if start:
            high = jnp.exp(high - top)
            total += jnp.sum(high, 0, keepdims=True)
            mixed += dot(v_ref[:, :start], high.astype(jnp.bfloat16), (1, 0))
        out_ref[:, start:stop] = (mixed / total).astype(jnp.bfloat16)
        log_ref[0, :, start:stop] = top + jnp.log(total)


def backward_kernel(q_ref, k_ref, v_ref, g_ref, o_ref, log_ref, dq_ref, dk_ref, dv_ref):
    rows = q_ref.shape[1]

    @pl.when(lax.rem(pl.program_id(0), GROUP) == 0)
    def _():
        dk_ref[...] = jnp.zeros_like(dk_ref)
        dv_ref[...] = jnp.zeros_like(dv_ref)

    key_rows = k_ref[...].T
    value_rows = v_ref[...].T
    for start in range(0, rows, QB):
        stop = start + QB
        query = q_ref[:, start:stop]
        grad = g_ref[:, start:stop]
        log_sum = log_ref[0, :, start:stop]
        centre = jnp.sum(
            grad.astype(jnp.float32) * o_ref[:, start:stop].astype(jnp.float32), 0, keepdims=True
        )
        grad_query = None
        for first, last in ((start, stop), (0, start)):
            if first == last:
                continue
            scores = dot(key_rows[first:last], query, (1, 0))
            if first == start:
                scores = diagonal(scores)
            prob = jnp.exp(scores - log_sum)
            grad_prob = dot(value_rows[first:last], grad, (1, 0))
            grad_score = (prob * (grad_prob - centre)).astype(jnp.bfloat16)
            part = dot(k_ref[:, first:last], grad_score, (1, 0))
            grad_query = part if grad_query is None else grad_query + part
            dk_ref[:, first:last] += dot(query, grad_score, (1, 1))
            dv_ref[:, first:last] += dot(grad, prob.astype(jnp.bfloat16), (1, 1))
        dq_ref[:, start:stop] = grad_query * SCALE


def attend_forward(query, key, value):
    rows = query.shape[1]
    head = pl.BlockSpec((HEAD_DIM, rows), lambda j: (j, 0))
    shared = pl.BlockSpec((HEAD_DIM, rows), lambda j: (j // GROUP, 0))
    return pl.pallas_call(
        forward_kernel,
        grid=(HEADS,),
        in_specs=[head, shared, shared],
        out_specs=[head, pl.BlockSpec((1, 1, rows), lambda j: (j, 0, 0))],
        out_shape=[
            jax.ShapeDtypeStruct((D, rows), jnp.bfloat16),
            jax.ShapeDtypeStruct((HEADS, 1, rows), jnp.float32),
        ],
        compiler_params=pltpu.CompilerParams(vmem_limit_bytes=VMEM),
        cost_estimate=pl.CostEstimate(
            flops=4 * HEADS * rows * rows * HEAD_DIM,
            bytes_accessed=8 * D * rows,
            transcendentals=HEADS * rows * rows // 2,
        ),
        name="attend_forward",
    )(query, key, value)


def attend_backward(query, key, value, grad, attn, log_sums):
    rows = query.shape[1]
    head = pl.BlockSpec((HEAD_DIM, rows), lambda j: (j, 0))
    shared = pl.BlockSpec((HEAD_DIM, rows), lambda j: (j // GROUP, 0))
    return pl.pallas_call(
        backward_kernel,
        grid=(HEADS,),
        in_specs=[
            head, shared, shared, head, head, pl.BlockSpec((1, 1, rows), lambda j: (j, 0, 0))
        ],
        out_specs=[head, shared, shared],
        out_shape=[
            jax.ShapeDtypeStruct((D, rows), jnp.float32),
            jax.ShapeDtypeStruct((KV, rows), jnp.float32),
            jax.ShapeDtypeStruct((KV, rows), jnp.float32),
        ],
        compiler_params=pltpu.CompilerParams(vmem_limit_bytes=VMEM),
        cost_estimate=pl.CostEstimate(
            flops=10 * HEADS * rows * rows * HEAD_DIM,
            bytes_accessed=16 * D * rows,
            transcendentals=HEADS * rows * rows // 2,
        ),
        name="attend_backward",
    )(query, key, value, grad, attn, log_sums)


def rope_tables(row_count):
    half = HEAD_DIM // 2
    position = jnp.arange(row_count, dtype=jnp.float32)
    frequency = THETA ** (-jnp.arange(half, dtype=jnp.float32) * 2.0 / HEAD_DIM)
    angle = frequency[:, None] * position[None, :]
    return (jnp.cos(angle), jnp.sin(angle))


def rotate(tensor, cosine, sine, direction):
    half = HEAD_DIM // 2
    rows = tensor.shape[1]
    split = tensor.reshape(-1, 2, half, rows)
    first_half, second_half = split[:, 0], split[:, 1]
    return jnp.stack(
        [
            first_half * cosine - direction * second_half * sine,
            second_half * cosine + direction * first_half * sine,
        ],
        1,
    ).reshape(tensor.shape)


def rms_norm(inputs, gain):
    scale_row = lax.rsqrt(jnp.mean(inputs * inputs, -1, keepdims=True) + EPS)
    normed = inputs * scale_row
    return (normed, scale_row, (normed * gain).astype(jnp.bfloat16))


def rms_back(grad_rows, normed, scale_row, gain):
    gain_grad = jnp.sum(grad_rows * normed, 0)
    weighted = grad_rows * gain
    return (
        gain_grad,
        scale_row * (weighted - normed * jnp.mean(weighted * normed, -1, keepdims=True)),
    )


def gather(weight):
    return lax.all_gather(weight, "shard", axis=0, tiled=True)


def scatter(grad):
    return lax.psum_scatter(grad, "shard", scatter_dimension=0, tiled=True)


def widen(totals):
    return [total.astype(jnp.float32) for total in totals]


def shards(
    tokens, lengths, cotangent, w_query, w_key, w_value, w_out, w_gate, w_up, w_down,
    gain_attn, gain_ffn,
):
    row_count = tokens.shape[0]
    low_type = jnp.bfloat16
    live_mask = (lax.iota(jnp.int32, row_count) < lengths[0]).astype(jnp.float32)[:, None]
    first = gather(
        jnp.concatenate([w_query, w_key, w_value, gain_attn[:, None], gain_ffn[:, None]], 1)
    )
    width = D + 2 * KV
    qkv_full = first[:, :width]
    gain_one = first[:, width].astype(jnp.float32)
    gain_two = first[:, width + 1].astype(jnp.float32)
    out_full = gather(w_out)
    gate_full = gather(w_gate)
    up_full = gather(w_up)
    down_full = gather(w_down)

    inputs = tokens.astype(jnp.float32)
    normed_one, scale_one, hidden_one = rms_norm(inputs, gain_one)
    cosine, sine = rope_tables(row_count)
    qkv = dot(qkv_full, hidden_one, (0, 1))
    query_rot = (rotate(qkv[:D], cosine, sine, 1.0).astype(low_type) * SCALE).astype(low_type)
    key_rot = rotate(qkv[D : D + KV], cosine, sine, 1.0).astype(low_type)
    values = qkv[D + KV :].astype(low_type)
    attn, log_sums = attend_forward(query_rot, key_rot, values)
    mixed = inputs + dot(attn, out_full, (0, 0))
    normed_two, scale_two, hidden_two = rms_norm(mixed, gain_two)
    gate = dot(hidden_two, gate_full, (1, 0))
    up_proj = dot(hidden_two, up_full, (1, 0))
    sigmoid_gate = jax.nn.sigmoid(gate)
    activated = gate * sigmoid_gate
    product_low = (activated * up_proj).astype(low_type)

    grad_rows = cotangent.astype(jnp.float32) * live_mask
    grad_low = grad_rows.astype(low_type)
    grad_down = dot(product_low, grad_low, (0, 0)).astype(low_type)
    grad_product = dot(grad_low, down_full, (1, 1)).astype(low_type).astype(jnp.float32)
    silu_slope = sigmoid_gate * (1.0 + gate * (1.0 - sigmoid_gate))
    grad_gate_act = (grad_product * up_proj * silu_slope).astype(low_type)
    grad_up_act = (grad_product * activated).astype(low_type)
    grad_gate = dot(hidden_two, grad_gate_act, (0, 0)).astype(low_type)
    grad_up = dot(hidden_two, grad_up_act, (0, 0)).astype(low_type)
    grad_gate_act, grad_up_act, grad_down, grad_gate, grad_up = lax.optimization_barrier(
        (grad_gate_act, grad_up_act, grad_down, grad_gate, grad_up)
    )
    early = lax.psum((scatter(grad_down), scatter(grad_gate), scatter(grad_up)), "rep")
    output = (mixed + dot(product_low, down_full, (1, 0))) * live_mask
    grad_hidden_two = dot(grad_gate_act, gate_full, (1, 1)) + dot(grad_up_act, up_full, (1, 1))
    grad_gain_two, grad_norm_two = rms_back(grad_hidden_two, normed_two, scale_two, gain_two)
    grad_mixed = grad_rows + grad_norm_two
    grad_branch = grad_mixed.astype(low_type)
    grad_out = dot(attn, grad_branch, (1, 0)).astype(low_type)
    grad_attn = dot(out_full, grad_branch, (1, 1)).astype(low_type)
    grad_query_rot, grad_key_rot, grad_val = attend_backward(
        query_rot, key_rot, values, grad_attn, attn, log_sums
    )
    grad_qkv = jnp.concatenate(
        [
            rotate(grad_query_rot, cosine, sine, -1.0).astype(low_type),
            rotate(grad_key_rot, cosine, sine, -1.0).astype(low_type),
            grad_val.astype(low_type),
        ],
        0,
    )
    grad_qkv_w = dot(hidden_one, grad_qkv, (0, 1))
    grad_hidden_one = dot(grad_qkv, qkv_full, (0, 1))
    grad_gain_one, grad_norm_one = rms_back(grad_hidden_one, normed_one, scale_one, gain_one)
    grad_inputs = grad_mixed + grad_norm_one
    last = jnp.concatenate(
        [grad_qkv_w, grad_gain_one[:, None], grad_gain_two[:, None]], 1
    )
    late = (scatter(grad_out), scatter(last.astype(low_type)))
    early, late = lax.optimization_barrier((early, late))
    total_down, total_gate, total_up = widen(early)
    total_out, total_last = widen(lax.psum(late, "rep"))
    return (
        output,
        grad_inputs,
        total_last[:, :D],
        total_last[:, D : D + KV],
        total_last[:, D + KV : width],
        total_out,
        total_gate,
        total_up,
        total_down,
        total_last[:, width],
        total_last[:, width + 1],
    )


def solution(mesh):
    placed = (
        P(("rep", "shard"), None),
        P(("rep", "shard")),
        P(("rep", "shard"), None),
        P("shard", None),
        P("shard", None),
        P("shard", None),
        P("shard", None),
        P("shard", None),
        P("shard", None),
        P("shard", None),
        P("shard"),
        P("shard"),
    )
    return jax.shard_map(
        shards,
        mesh=mesh,
        in_specs=placed,
        out_specs=(
            P(("rep", "shard"), None),
            P(("rep", "shard"), None),
            P("shard", None),
            P("shard", None),
            P("shard", None),
            P("shard", None),
            P("shard", None),
            P("shard", None),
            P("shard", None),
            P("shard"),
            P("shard"),
        ),
        check_vma=False,
    )
```

time: 1590 us -> 747 us (0.47)
  matrix products: 841 us -> 170 us
  blocking collectives: 422 us -> 0 us
  waiting for transfers between devices: 161 us -> 360 us
  Pallas kernels: 0 us -> 117 us
  other arithmetic: 99.4 us -> 37.1 us
    dot_general x42 -> x15, matrix products: 841 us -> 170 us  [dot(): lax.dot_general(left, right, ((contract[:1], contract[1:]), ((), ())), pr...]
    psum x1 -> x0, blocking collectives: 388 us -> none  [shards(): lax.psum((shares[0], shares[1], shares[2], shares[3], shares[4], shares[5...]
    psum x0 -> x2, waiting for transfers between devices: none -> 221 us  [the longest x1 149 us: shards(): lax.psum((scatter(grad_down), scatter(grad_gate), scatter(grad_up)), 'rep')]
    pallas_call x0 -> x2, Pallas kernels: none -> 117 us  [the longest x1 68.8 us: attend_backward(): pl.pallas_call(backward_kernel, grid=(HEADS,), in_specs=[head, shared, sh...]
    all_gather x5, waiting for transfers between devices: 0.05 us -> 64.6 us  [gather(): return lax.all_gather(weight, 'shard', axis=0, tiled=True)]
    reduce_sum x3 -> x0, other arithmetic: 64.2 us -> none  [visit(): summed = jnp.sum(raised, -1, keepdims=True)]
    unnamed x15 -> x13, waiting for transfers between devices: 57.1 us -> 3.94 us
    reduce_scatter x4, waiting for transfers between devices: 104 us -> 70.2 us  [scatter(): return lax.psum_scatter(grad, 'shard', scatter_dimension=0, tiled=True)]
  transfers between devices with their start and end apart: 12 -> 12, of which waited for: 4 -> 8; matrix products, arithmetic and copies ran while one was open for 23% -> 21% of each run, Pallas kernels for 0% -> 16%
where the time goes in v1:
time: 747 us; the launch traced here: 739 us
  waiting for transfers between devices  360 us (48%)
  matrix products  170 us (23%)
  Pallas kernels  117 us (16%)
  local copies, waits for them, and re-layouts  37.6 us (5%)
  other arithmetic  37.1 us (5%)
  between operations  15.8 us (2%)
    dot_general x15, matrix products, dot(): lax.dot_general(left, right, ((contract[:1], contract[1:]), ((), ())), pr...  170 us
    psum x1, waiting for transfers between devices, shards(): lax.psum((scatter(grad_down), scatter(grad_gate), scatter(grad_up)), 'rep')  149 us
    psum x1, waiting for transfers between devices, shards(): total_out, total_last = widen(lax.psum(late, 'rep'))  72.3 us
    reduce_scatter x4, waiting for transfers between devices, scatter(): return lax.psum_scatter(grad, 'shard', scatter_dimension=0, tiled=True)  70.2 us
    pallas_call x1, Pallas kernels, attend_backward(): pl.pallas_call(backward_kernel, grid=(HEADS,), in_specs=[head, shared, sh...  68.8 us
    all_gather x5, waiting for transfers between devices, gather(): return lax.all_gather(weight, 'shard', axis=0, tiled=True)  64.6 us
    pallas_call x1, Pallas kernels, attend_forward(): pl.pallas_call(forward_kernel, grid=(HEADS,), in_specs=[head, shared, sha...  48.6 us
    unnamed x68, local copies, waits for them, and re-layouts  22.4 us
  transfers between devices with their start and end apart: 12, of which 8 were waited for; matrix products, arithmetic and copies ran while one was open for 21% of the time, Pallas kernels for 16%

profile of v1, /device:TPU:0, one launch (start us, length us, event | category | flops | bytes accessed | tf_op | source)
XLA Modules:
  0.0 739.0 jit_solution(9053403037123449378)
XLA Ops:
  7.2 0.9 broadcast_in_dim.14
  8.1 0.8 broadcast_in_dim.15
  8.9 1.1 copy.35
  10.0 1.1 copy.36
  11.1 2.0 concatenate.10
  13.1 0.7 all-gather.8.cloned.1.call-update
  13.9 0.7 all-gather.10.cloned.1.call-update
  14.6 0.5 all-gather.14.cloned.1.call-update
  15.2 0.5 all-gather.12.cloned.1.call-update
  16.5 0.6 fusion.14
  17.1 1.5 broadcast_multiply_fusion
  18.6 26.2 %all-gather.6.cloned.1.call-done = bf16[960,1602]{1,0:T(8,128)(2,1)} async-done(((bf16[240,1602]{1,0:T(8,128)(2,1)}), bf16[960,1602]{1,0:T(8,128)(2,1)}) %all-gather.6.cloned.1.call-update) | async-done | bytes 3075856 | tf_op jit(solution)/shard_map/all_gather | solution.py:178
  44.7 1.4 convert_reduce_fusion
  46.2 7.4 %fusion.19 = f32[1600,1536]{1,0:T(8,128)S(1)} fusion(bf16[960,1602]{1,0:T(8,128)(2,1)} %all-gather.6.cloned.1.call-done, bf16[1536,960]{0,1:T(8,128)(2,1)S(1)} %copy-done.8, f32[960]{0:T(1024)S(1)} %get-tuple-element.79, f32[1536]{0:T(1024)S(1)} %add_rsqrt_fusion.1), kind=kOutput, calls=%fused_computation.47 | convolution fusion | flops 4724490240 | bytes 15865344 | tf_op jit(solution)/shard_map/dot_general | solution.py:23
  54.2 3.2 copy-done.10
  57.5 1.0 subtract_convert_fusion.1
  58.4 0.6 slice-done.2
  59.4 2.0 maximum_multiply_fusion
  61.4 48.6 %attend_forward.1 = (bf16[960,1536]{1,0:T(8,128)(2,1)S(1)}, f32[15,1,1536]{2,1,0:T(1,128)S(1)}) custom-call(bf16[960,1536]{1,0:T(8,128)(2,1)} %bitcast.41, bf16[320,1536]{1,0:T(8,128)(2,1)S(1)} %bitcast.34, bf16[320,1536]{1,0:T(8,128)(2,1)S(1)} %slice.121.v_ref), custom_call_target="tpu_custom_call" | custom-call | flops 9059696640 | bytes 11796480 | tf_op jit(solution)/shard_map/attend_forward/pallas_call | solution.py:95
  110.0 7.3 multiply_reduce_fusion.2
  117.4 2.9 copy-done.6
  120.2 2.1 multiply_convert_fusion.1
  122.4 14.5 %fusion.33 = f32[1536,2560]{1,0:T(8,128)} fusion(bf16[1536,960]{0,1:T(8,128)(2,1)} %multiply_convert_fusion.1, bf16[960,2560]{1,0:T(8,128)(2,1)} %all-gather.10.cloned.1.call-done), kind=kOutput, calls=%fused_computation.77 | convolution fusion | flops 7549747200 | bytes 23592960 | tf_op jit(solution)/shard_map/dot_general | solution.py:23
  136.9 11.6 %all-gather.14.cloned.1.call-done = bf16[2560,960]{0,1:T(8,128)(2,1)} async-done(((bf16[640,960]{0,1:T(8,128)(2,1)}), bf16[2560,960]{0,1:T(8,128)(2,1)}) %all-gather.14.cloned.1.call-update) | async-done | bytes 4915216 | tf_op jit(solution)/shard_map/all_gather | solution.py:178
  148.5 13.2 %convolution_convert_fusion = bf16[1536,2560]{1,0:T(8,128)(2,1)} fusion(bf16[2560,960]{0,1:T(8,128)(2,1)} %all-gather.14.cloned.1.call-done, bf16[1536,960]{0,1:T(8,128)(2,1)S(1)} %copy-done.13, f32[1536]{0:T(1024)S(1)} %fusion.29), kind=kOutput, calls=%fused_computation.8 | convolution fusion | flops 7558103040 | bytes 15734784 | tf_op jit(solution)/shard_map/dot_general | solution.py:23
  161.7 26.8 %all-gather.12.cloned.1.call-done = bf16[960,2560]{1,0:T(8,128)(2,1)} async-done(((bf16[240,2560]{1,0:T(8,128)(2,1)}), bf16[960,2560]{1,0:T(8,128)(2,1)}) %all-gather.12.cloned.1.call-update) | async-done | bytes 4915216 | tf_op jit(solution)/shard_map/all_gather | solution.py:178
  188.5 24.2 %fusion.1 = (bf16[1536,2560]{1,0:T(8,128)(2,1)S(1)}, bf16[1536,2560]{1,0:T(8,128)(2,1)}, bf16[1536,2560]{1,0:T(8,128)(2,1)}) fusion(bf16[1536,2560]{1,0:T(8,128)(2,1)} %convolution_convert_fusion, f32[1536,2560]{1,0:T(8,128)} %fusion.33, bf16[1536,960]{0,1:T(8,128)(2,1)} %multiply_convert_fusion.1, bf16[960,2560]{1,0:T(8,128)(2,1)} %all-gather.12.cloned.1.call-done), kind=kOutput, calls=%fused_computation.3 | convolution fusion | flops 7612661760 | bytes 55050240 | tf_op jit(solution)/shard_map/dot_general | solution.py:23
  212.7 15.5 %convolution_convert_fusion.1 = bf16[2560,960]{0,1:T(8,128)(2,1)} fusion(bf16[1536,2560]{1,0:T(8,128)(2,1)} %get-tuple-element.88, bf16[1536,960]{0,1:T(8,128)(2,1)S(1)} %copy-done.13, f32[1536]{0:T(1024)S(1)} %fusion.29), kind=kOutput, calls=%fused_computation.31 | convolution fusion | flops 7556628480 | bytes 15734784 | tf_op jit(solution)/shard_map/dot_general | solution.py:23
  228.2 9.3 %convolution_convert_fusion.3 = bf16[960,2560]{1,0:T(8,128)(2,1)} fusion(bf16[1536,960]{0,1:T(8,128)(2,1)S(1)} %copy-done.14, bf16[1536,2560]{1,0:T(8,128)(2,1)S(1)} %get-tuple-element.27), kind=kOutput, calls=%fused_computation.33 | convolution fusion | flops 7552204800 | bytes 15728640 | tf_op jit(solution)/shard_map/dot_general | solution.py:23
  237.5 12.5 %convolution_convert_fusion.2 = bf16[960,2560]{1,0:T(8,128)(2,1)} fusion(bf16[1536,960]{0,1:T(8,128)(2,1)} %multiply_convert_fusion.1, bf16[1536,2560]{1,0:T(8,128)(2,1)} %get-tuple-element.28), kind=kOutput, calls=%fused_computation.32 | convolution fusion | flops 7552204800 | bytes 15728640 | tf_op jit(solution)/shard_map/dot_general | solution.py:23
  250.0 7.9 %copy.43 = bf16[2560,960]{1,0:T(8,128)(2,1)} copy(bf16[2560,960]{0,1:T(8,128)(2,1)} %convolution_convert_fusion.1) | data formatting | bytes 9830400
  257.9 0.7 reduce-scatter.8.cloned.1.call-update
  258.7 0.7 reduce-scatter.10.cloned.1.call-update
  259.4 11.9 %fusion.34 = f32[1536,960]{0,1:T(8,128)S(1)} fusion(bf16[1536,2560]{1,0:T(8,128)(2,1)} %copy-done.28, bf16[960,2560]{1,0:T(8,128)(2,1)} %all-gather.10.cloned.1.call-done), kind=kOutput, calls=%fused_computation.78 | convolution fusion | flops 7549747200 | bytes 18677760 | tf_op jit(solution)/shard_map/dot_general | solution.py:23
  271.4 14.8 %multiply_reduce_fusion = (bf16[960]{0:T(1024)(128)(2,1)S(1)}, f32[1536]{0:T(1024)S(1)}, f32[1536,960]{0,1:T(8,128)}) fusion(f32[1536,960]{0,1:T(8,128)} %copy-done.6, f32[1536]{0:T(1024)S(1)} %add_rsqrt_fusion, f32[960]{0:T(1024)S(1)} %get-tuple-element.78, f32[1536,960]{0,1:T(8,128)S(1)} %fusion.34, bf16[1536,2560]{1,0:T(8,128)(2,1)} %get-tuple-element.28, ...), kind=kOutput, calls=%fused_computation.23 | convolution fusion | flops 7560066560 | bytes 30492288 | tf_op jit(solution)/shard_map/dot_general | solution.py:23
  286.4 4.3 multiply_add_fusion
  290.8 4.7 fusion.16.g_ref
  295.6 68.8 %attend_backward.1 = (f32[960,1536]{1,0:T(8,128)}, f32[320,1536]{1,0:T(8,128)S(1)}, f32[320,1536]{1,0:T(8,128)S(1)}) custom-call(bf16[960,1536]{1,0:T(8,128)(2,1)} %bitcast.42, bf16[320,1536]{1,0:T(8,128)(2,1)S(1)} %bitcast.35, bf16[320,1536]{1,0:T(8,128)(2,1)S(1)} %copy-done.1, bf16[960,1536]{1,0:T(8,128)(2,1)} %fusion.16.g_ref, ...), custom_call_target="tpu_custom_call" | custom-call | flops 22649241600 | bytes 23592960 | tf_op jit(solution)/shard_map/attend_backward/pallas_call | solution.py:118
  364.4 1.0 convert_element_type.134
  365.7 1.0 pad_maximum_fusion.5
  366.8 4.4 convolution_convert_fusion.6
  371.5 4.9 subtract_convert_fusion
  376.7 1.5 copy-done.9
  378.7 8.3 %fusion.13 = (bf16[960]{0:T(1024)(128)(2,1)S(1)}, f32[1536]{0:T(1024)S(1)}, f32[1536,960]{0,1:T(8,128)}) fusion(bf16[1536,960]{0,1:T(8,128)(2,1)S(1)} %copy-done.9, f32[1536]{0:T(1024)S(1)} %copy-done.24, f32[960]{0:T(1024)S(1)} %copy-done.26, bf16[320,1536]{1,0:T(8,128)(2,1)S(1)} %copy-done.19, bf16[320,1536]{1,0:T(8,128)(2,1)S(1)} %bitcast.45, ...), kind=kOutput, calls=%fused_computation.21 | convolution fusion | flops 4743656960 | bytes 16856448 | tf_op jit(solution)/shard_map/dot_general | solution.py:23
  387.3 7.2 convolution_convert_fusion.4
  394.5 6.0 concatenate.12
  400.6 2.4 copy.44
  403.0 10.3 %reduce-scatter.10.cloned.1.call-done = bf16[240,2560]{1,0:T(8,128)(2,1)} async-done(((bf16[960,2560]{1,0:T(8,128)(2,1)}), bf16[240,2560]{1,0:T(8,128)(2,1)}) %reduce-scatter.10.cloned.1.call-update) | async-done | bytes 1228816 | tf_op jit(solution)/shard_map/reduce_scatter | solution.py:182
  413.6 14.5 %add_multiply_fusion = f32[1536,960]{0,1:T(8,128)} fusion(f32[1536,960]{0,1:T(8,128)} %copy-done.6, bf16[1536,2560]{1,0:T(8,128)(2,1)} %get-tuple-element.88, bf16[2560,960]{0,1:T(8,128)(2,1)} %all-gather.14.cloned.1.call-done, f32[1536]{0:T(1024)S(1)} %fusion.29), kind=kOutput, calls=%fused_computation.28 | convolution fusion | flops 7552696320 | bytes 24582144 | tf_op jit(solution)/shard_map/dot_general | solution.py:23
  428.1 19.2 %reduce-scatter.12.cloned.1.call-done = bf16[240,960]{1,0:T(8,128)(2,1)} async-done(((bf16[960,960]{1,0:T(8,128)(2,1)}), bf16[240,960]{1,0:T(8,128)(2,1)}) %reduce-scatter.12.cloned.1.call-update) | async-done | bytes 460816 | tf_op jit(solution)/shard_map/reduce_scatter | solution.py:182
  447.3 40.7 %reduce-scatter.14.cloned.1.call-done = bf16[240,1602]{1,0:T(8,128)(2,1)} async-done(((bf16[960,1602]{1,0:T(8,128)(2,1)}), bf16[240,1602]{1,0:T(8,128)(2,1)}) %reduce-scatter.14.cloned.1.call-update) | async-done | bytes 768976 | tf_op jit(solution)/shard_map/reduce_scatter | solution.py:182
  488.0 149.2 %all-reduce.7.cloned.1.call-done = (bf16[640,960]{0,1:T(8,128)(2,1)}, bf16[240,2560]{1,0:T(8,128)(2,1)}, bf16[240,2560]{1,0:T(8,128)(2,1)}) async-done(((bf16[640,960]{0,1:T(8,128)(2,1)}, bf16[240,2560]{1,0:T(8,128)(2,1)}, bf16[240,2560]{1,0:T(8,128)(2,1)}), (bf16[640,960]{0,1:T(8,128)(2,1)}, bf16[240,2560]{1,0:T(8,128)(2,1)}, bf16[240,2560]{1,0:T(8,128)(2,1)})) %all-reduce.7.cloned.1.call-update) | async-done | bytes 3686416 | tf_op jit(solution)/shard_map/psum | solution.py:236
  637.2 8.9 %fusion.12 = f32[1536,960]{0,1:T(8,128)} fusion(f32[1536,960]{0,1:T(8,128)} %copy-done.7, bf16[1536,960]{0,1:T(8,128)(2,1)S(1)} %copy-done.9, f32[1536,960]{0,1:T(8,128)} %get-tuple-element.106, f32[1536]{0:T(1024)S(1)} %broadcast_multiply_fusion.1, f32[960]{0:T(1024)S(1)} %copy-done.26, f32[1536]{0:T(1024)S(1)} %copy-done.24), kind=kLoop, calls=%fused_computation.20 | loop fusion | flops 10321920 | bytes 20659968 | tf_op jit(solution)/shard_map/add | solution.py:258
  646.1 1.7 convert_element_type.138
  647.8 1.7 convert_element_type.139
  649.6 1.6 convert_element_type.140
  651.2 72.3 %all-reduce.5.cloned.1.call-done = (bf16[240,1602]{1,0:T(8,128)(2,1)}, bf16[240,960]{1,0:T(8,128)(2,1)}) async-done(((bf16[240,1602]{1,0:T(8,128)(2,1)}, bf16[240,960]{1,0:T(8,128)(2,1)}), (bf16[240,1602]{1,0:T(8,128)(2,1)}, bf16[240,960]{1,0:T(8,128)(2,1)})) %all-reduce.5.cloned.1.call-update) | async-done | bytes 1229776 | tf_op jit(solution)/shard_map/psum | solution.py:265
  723.5 1.2 fusion.32
  724.7 2.1 slice.91
  726.8 1.2 convert_element_type.136
  728.1 1.1 convert_element_type.137
  729.1 0.9 copy.42
  730.0 0.9 copy.41
  730.9 0.8 slice_reduce_fusion
  (97 shorter events, 3.6 us)
Async XLA Ops:
  7.2 9.3 %copy-start.8 = (bf16[1536,960]{0,1:T(8,128)(2,1)S(1)}, bf16[1536,960]{0,1:T(8,128)(2,1)}, u32[]{:S(2)}) copy-start(bf16[1536,960]{0,1:T(8,128)(2,1)} %param.12) | copy-start | bytes 8847364
  7.2 37.6 %all-gather.6.cloned.1.call-start = ((), (), s32[]{:S(2)}) async-start(), calls=%async_computation.5 | async-start | bytes 3993600 | tf_op jit(solution)/shard_map/all_gather | solution.py:178
  13.1 97.0 %all-gather.8.cloned.1.call-start = ((), (), s32[]{:S(2)}) async-start(), calls=%async_computation.6 | async-start | bytes 2457600 | tf_op jit(solution)/shard_map/all_gather | solution.py:178
  13.8 108.6 %all-gather.10.cloned.1.call-start = ((), (), s32[]{:S(2)}) async-start(), calls=%async_computation.7 | async-start | bytes 6144000 | tf_op jit(solution)/shard_map/all_gather | solution.py:178
  14.6 133.9 %all-gather.14.cloned.1.call-start = ((), (), s32[]{:S(2)}) async-start(), calls=%async_computation.9 | async-start | bytes 6144000 | tf_op jit(solution)/shard_map/all_gather | solution.py:178
  15.1 173.3 %all-gather.12.cloned.1.call-start = ((), (), s32[]{:S(2)}) async-start(), calls=%async_computation.8 | async-start | bytes 6144000 | tf_op jit(solution)/shard_map/all_gather | solution.py:178
  15.7 384.9 %reduce-scatter.16.cloned.1.call-start = ((), (), s32[]{:S(2)}) async-start(), calls=%async_computation.14 | async-start | bytes 6553600
  17.1 36.5 %copy-start.23 = (f32[1536]{0:T(1024)}, f32[1536]{0:T(1024)S(1)}, u32[]{:S(2)}) copy-start(f32[1536]{0:T(1024)S(1)} %add_rsqrt_fusion.1) | copy-start | bytes 18436
  18.6 39.9 %copy-start.11 = (f32[32,1536]{1,0:T(8,128)}, f32[32,1536]{1,0:T(8,128)S(1)}, u32[]{:S(2)}) copy-start(f32[32,1536]{1,0:T(8,128)S(1)} %get-tuple-element.102) | copy-start | bytes 589828
  46.2 7.5 %copy-start.25 = (f32[960]{0:T(1024)}, f32[960]{0:T(1024)S(1)}, u32[]{:S(2)}) copy-start(f32[960]{0:T(1024)S(1)} %get-tuple-element.79) | copy-start | bytes 11524
  53.7 3.8 copy-start.10
  53.8 7.6 %copy-start = (bf16[320,1536]{1,0:T(8,128)(2,1)}, bf16[320,1536]{1,0:T(8,128)(2,1)S(1)}, u32[]{:S(2)}) copy-start(bf16[320,1536]{1,0:T(8,128)(2,1)S(1)} %slice.121.v_ref) | copy-start | bytes 2949124
  57.5 1.5 slice-start.2
  59.4 2.0 copy-start.2
  110.0 7.3 copy-start.4
  117.4 2.9 copy-start.6
  122.4 26.1 %copy-start.13 = (bf16[1536,960]{0,1:T(8,128)(2,1)S(1)}, bf16[1536,960]{0,1:T(8,128)(2,1)}, u32[]{:S(2)}) copy-start(bf16[1536,960]{0,1:T(8,128)(2,1)} %param.14) | copy-start | bytes 8847364
  212.7 15.5 %copy-start.28 = (bf16[1536,2560]{1,0:T(8,128)(2,1)}, bf16[1536,2560]{1,0:T(8,128)(2,1)S(1)}, u32[]{:S(2)}) copy-start(bf16[1536,2560]{1,0:T(8,128)(2,1)S(1)} %get-tuple-element.27) | copy-start | bytes 23592964
  212.7 15.5 %copy-start.14 = (bf16[1536,960]{0,1:T(8,128)(2,1)S(1)}, bf16[1536,960]{0,1:T(8,128)(2,1)}, u32[]{:S(2)}) copy-start(bf16[1536,960]{0,1:T(8,128)(2,1)} %multiply_convert_fusion.1) | copy-start | bytes 8847364
  257.9 145.1 %reduce-scatter.8.cloned.1.call-start = ((), (), s32[]{:S(2)}) async-start(), calls=%async_computation.10 | async-start | bytes 6144000 | tf_op jit(solution)/shard_map/reduce_scatter | solution.py:182
  258.6 154.7 %reduce-scatter.10.cloned.1.call-start = ((), (), s32[]{:S(2)}) async-start(), calls=%async_computation.11 | async-start | bytes 6144000 | tf_op jit(solution)/shard_map/reduce_scatter | solution.py:182
  259.4 187.9 %reduce-scatter.12.cloned.1.call-start = ((), (), s32[]{:S(2)}) async-start(), calls=%async_computation.12 | async-start | bytes 2457600 | tf_op jit(solution)/shard_map/reduce_scatter | solution.py:182
  259.4 27.0 %slice-start = ((s8[5898240]{0:T(1024)(128)(4,1)}), s8[4194304]{0:T(1024)(128)(4,1)S(1)}, s32[]{:S(2)}) async-start(s8[5898240]{0:T(1024)(128)(4,1)} %bitcast.36), calls=%async_computation.17 | async-start | bytes 8388608
  271.4 15.0 %slice-start.1 = ((s8[5898240]{0:T(1024)(128)(4,1)}), s8[1703936]{0:T(1024)(128)(4,1)S(1)}, s32[]{:S(2)}) async-start(s8[5898240]{0:T(1024)(128)(4,1)} %bitcast.36), calls=%async_computation.18 | async-start | bytes 3407872
  286.4 4.4 copy-start.27
  290.8 76.0 %copy-start.7 = (f32[1536,960]{0,1:T(8,128)}, f32[1536,960]{0,1:T(8,128)S(1)}, u32[]{:S(2)}) copy-start(f32[1536,960]{0,1:T(8,128)S(1)} %multiply_add_fusion) | copy-start | bytes 17694724
  290.8 4.7 copy-start.1
  290.8 4.7 copy-start.3
  295.5 69.9 %copy-start.12 = (f32[32,1536]{1,0:T(8,128)S(1)}, f32[32,1536]{1,0:T(8,128)}, u32[]{:S(2)}) copy-start(f32[32,1536]{1,0:T(8,128)} %copy-done.11) | copy-start | bytes 589828
  295.5 69.9 %copy-start.15 = (f32[32,1536]{1,0:T(8,128)S(1)}, f32[32,1536]{1,0:T(8,128)}, u32[]{:S(2)}) copy-start(f32[32,1536]{1,0:T(8,128)} %get-tuple-element.100) | copy-start | bytes 589828
  364.4 2.4 copy-start.5
  371.2 116.7 %reduce-scatter.14.cloned.1.call-start = ((), (), s32[]{:S(2)}) async-start(), calls=%async_computation.13 | async-start | bytes 3993600 | tf_op jit(solution)/shard_map/reduce_scatter | solution.py:182
  371.5 5.2 copy-start.22
  376.4 1.9 copy-start.9
  376.4 2.1 copy-start.19
  376.4 2.3 copy-start.20
  376.4 2.3 copy-start.24
  376.4 2.3 copy-start.26
  400.5 236.6 %all-reduce.7.cloned.1.call-start = ((), (), s32[]{:S(2)}) async-start(), calls=%async_computation.16 | async-start | bytes 7372800 | tf_op jit(solution)/shard_map/psum | solution.py:236
  413.3 310.2 %all-reduce.5.cloned.1.call-start = ((), (), s32[]{:S(2)}) async-start(), calls=%async_computation.15 | async-start | bytes 2580480 | tf_op jit(solution)/shard_map/psum | solution.py:265
  637.2 8.9 %copy-start.18 = (bf16[240,2560]{1,0:T(8,128)(2,1)S(1)}, bf16[240,2560]{1,0:T(8,128)(2,1)}, u32[]{:S(2)}) copy-start(bf16[240,2560]{1,0:T(8,128)(2,1)} %get-tuple-element.38) | copy-start | bytes 3686404
  637.2 10.7 %copy-start.17 = (bf16[240,2560]{1,0:T(8,128)(2,1)S(1)}, bf16[240,2560]{1,0:T(8,128)(2,1)}, u32[]{:S(2)}) copy-start(bf16[240,2560]{1,0:T(8,128)(2,1)} %get-tuple-element.39) | copy-start | bytes 3686404
  646.1 3.5 copy-start.16
  723.5 4.5 copy-start.21
Sparse Core Ops, SparseCore 0:
  13.2 31.5 all-gather.5
  46.3 21.8 all-gather.7
  69.8 38.5 all-gather.9
  109.8 38.6 all-gather.13
  149.9 38.5 all-gather.11
  258.0 51.3 reduce-scatter.15
  312.2 49.2 reduce-scatter.7
  364.0 49.2 reduce-scatter.9
  416.6 30.6 reduce-scatter.11
  449.7 38.2 reduce-scatter.13
  493.0 144.0 all-reduce.6
  641.0 82.4 all-reduce.4
